TPU v7x, 32 devices: a whole 2x2x4 slice. The times are simulated.
32 devices in a mesh: grp: 2 (over y), ex: 8 (over z, x), dim: 2 (over core).
Axes of the slice: x: 2, y: 2, z: 4, core: 2. Of those that a mesh axis runs over, the one named last changes fastest.
Arguments:
- queries: bfloat16 [48, 16384], P('ex', 'dim'), may hold values from -6 to 6
- train_grads: bfloat16 [2048, 16384], P(('grp', 'ex'), 'dim'), parts along dimension 0, may hold values from -0.046875 to 0.046875
- precond: bfloat16 [16384, 64], P('dim'), may hold values from -0.03 to 3, as said below
Outputs:
- scores: float32 [2048, 48], P(('grp', 'ex'), 'dim'), parts along dimension 0
There are 2 independent parts, one for each index of `grp`. A program takes and returns all parts, laid end to end along the dimension named above; an argument that names none is the same for every part. Nothing has to cross between parts.
Inputs may be any that keep to these rules, and one draw needn't show every extreme that they name: `precond`: entries of the preconditioner blocks.
All inputs are finite; a program needn't handle non-finite values.
Results may differ from a plain program's by a relative error of at most 0.0029.
Values may be sent and summed in bfloat16 or wider, within the bound.
No kernel may reach another device: no remote copies, remote signals or barrier semaphores. Data moves between devices by JAX's collectives and lax.ppermute only.
A program may use at most 64 MiB of HBM per device.

v0:
```python
import math

import jax
import jax.numpy as jnp
from jax import lax
from jax.sharding import PartitionSpec as P


def shifted(block, axis, distance):
    devices = range(lax.axis_size(axis))
    route = [((i - distance) % len(devices), i) for i in devices]
    return lax.ppermute(block, axis, route)


def per_device(queries, train_grads, precond):
    cycle_size = lax.axis_size("ex")
    dim_size = lax.axis_size("dim")
    query_rows, dims_dev = queries.shape
    train_rows = train_grads.shape[0]
    block_size = precond.shape[1]
    all_queries = query_rows * cycle_size
    matrices = precond.reshape(dims_dev // block_size, block_size, block_size)
    grouped = queries.reshape(query_rows, dims_dev // block_size, block_size)
    own_rows = jnp.einsum("qbi,bij->qbj", grouped, matrices, preferred_element_type=jnp.float32)
    own_rows = own_rows.reshape(query_rows, dims_dev).astype(jnp.bfloat16)
    contract = (((1,), (1,)), ((), ()))
    empty = jnp.zeros((train_rows, all_queries), jnp.float32)
    group_len = math.gcd(cycle_size, 8)
    my_index = lax.axis_index("ex")

    def advance(moving):
        return shifted(moving, "ex", 1)

    def score_group(running, held, first_step):
        joined = jnp.concatenate(held, 0)
        score_tile = lax.dot_general(
            train_grads, joined, contract, preferred_element_type=jnp.float32
        )
        for offset in range(group_len):
            source = (my_index - first_step - offset) % cycle_size
            running = lax.dynamic_update_slice(
                running,
                score_tile[:, offset * query_rows : (offset + 1) * query_rows],
                (jnp.int32(0), source * query_rows),
            )
        return running

    moving = own_rows
    held = [moving]
    for offset in range(1, group_len):
        moving = advance(moving)
        held.append(moving)
    running = score_group(empty, held, jnp.int32(0))

    def cycle_step(group, carry):
        moving, running = carry
        held = []
        for offset in range(group_len):
            moving = advance(moving)
            held.append(moving)
        return (moving, score_group(running, held, (group * group_len).astype(jnp.int32)))

    moving, partial_value = lax.fori_loop(1, cycle_size // group_len, cycle_step, (moving, running))
    summed = lax.psum(partial_value, "dim")
    half_cols = all_queries // dim_size
    return lax.dynamic_slice_in_dim(summed, lax.axis_index("dim") * half_cols, half_cols, 1)


def solution(mesh):
    placed = (P("ex", "dim"), P(("grp", "ex"), "dim"), P("dim", None))
    return jax.shard_map(
        per_device, mesh=mesh, in_specs=placed, out_specs=P(("grp", "ex"), "dim"), check_vma=False
    )
```

profile of v0, /device:TPU:0, one launch (start us, length us, event | category | flops | bytes accessed | tf_op | source)
XLA Modules:
  0.0 74.7 jit_solution(8000009928762320291)
XLA Ops:
  0.0 2.9 %copy.9 = bf16[8192,64]{1,0:T(8,128)(2,1)} copy(bf16[8192,64]{0,1:T(8,128)(2,1)} %param.5) | data formatting | bytes 2097152 | tf_op jit(solution)/shard_map/reshape | solution.py:22
  2.9 0.2 reshape.9
  3.1 2.2 %fusion = bf16[6,128,64]{2,0,1:T(8,128)(2,1)S(1)} fusion(bf16[128,64,64]{2,1,0:T(8,128)(2,1)} %bitcast.8, bf16[6,128,64]{2,1,0:T(8,128)(2,1)S(1)} %reshape.9), kind=kOutput, calls=%fused_computation.1 | convolution fusion | flops 6340608 | bytes 1245184 | tf_op jit(solution)/shard_map/qbi,bij->qbj/dot_general | solution.py:24
  5.4 0.2 convert_element_type.11
  5.6 3.0 %collective-permute-start = (bf16[6,8192]{1,0:T(8,128)(2,1)S(1)}, bf16[6,8192]{1,0:T(8,128)(2,1)S(1)}, u32[]{:S(2)}, u32[]{:S(2)}) collective-permute-start(bf16[6,8192]{1,0:T(8,128)(2,1)S(1)} %convert_element_type.11), channel_id=1, source_target_pairs={{14,0},{0,2},{2,4},{4,6},{6,8},{8,10},{10,12},{12,14},{15,1},{1,3}... | collective-permute-start | bytes 294920 | tf_op jit(solution)/shard_map/ppermute | solution.py:12
  8.6 6.5 %collective-permute-done = bf16[6,8192]{1,0:T(8,128)(2,1)S(1)} collective-permute-done((bf16[6,8192]{1,0:T(8,128)(2,1)S(1)}, bf16[6,8192]{1,0:T(8,128)(2,1)S(1)}, u32[]{:S(2)}, u32[]{:S(2)}) %collective-permute-start) | collective-permute-done | bytes 98336 | tf_op jit(solution)/shard_map/ppermute | solution.py:12
  15.1 0.0 collective-permute-start.1
  15.1 7.7 %collective-permute-done.1 = bf16[6,8192]{1,0:T(8,128)(2,1)S(1)} collective-permute-done((bf16[6,8192]{1,0:T(8,128)(2,1)S(1)}, bf16[6,8192]{1,0:T(8,128)(2,1)S(1)}, u32[]{:S(2)}, u32[]{:S(2)}) %collective-permute-start.1) | collective-permute-done | bytes 98336 | tf_op jit(solution)/shard_map/ppermute | solution.py:12
  22.8 0.0 collective-permute-start.2
  22.8 7.7 %collective-permute-done.2 = bf16[6,8192]{1,0:T(8,128)(2,1)S(1)} collective-permute-done((bf16[6,8192]{1,0:T(8,128)(2,1)S(1)}, bf16[6,8192]{1,0:T(8,128)(2,1)S(1)}, u32[]{:S(2)}, u32[]{:S(2)}) %collective-permute-start.2) | collective-permute-done | bytes 98336 | tf_op jit(solution)/shard_map/ppermute | solution.py:12
  30.5 0.0 collective-permute-start.3
  30.5 7.7 %collective-permute-done.3 = bf16[6,8192]{1,0:T(8,128)(2,1)S(1)} collective-permute-done((bf16[6,8192]{1,0:T(8,128)(2,1)S(1)}, bf16[6,8192]{1,0:T(8,128)(2,1)S(1)}, u32[]{:S(2)}, u32[]{:S(2)}) %collective-permute-start.3) | collective-permute-done | bytes 98336 | tf_op jit(solution)/shard_map/ppermute | solution.py:12
  38.1 0.0 collective-permute-start.4
  38.1 7.7 %collective-permute-done.4 = bf16[6,8192]{1,0:T(8,128)(2,1)S(1)} collective-permute-done((bf16[6,8192]{1,0:T(8,128)(2,1)S(1)}, bf16[6,8192]{1,0:T(8,128)(2,1)S(1)}, u32[]{:S(2)}, u32[]{:S(2)}) %collective-permute-start.4) | collective-permute-done | bytes 98336 | tf_op jit(solution)/shard_map/ppermute | solution.py:12
  45.8 0.6 copy-done.1
  46.4 0.0 collective-permute-start.5
  46.4 8.8 %collective-permute-done.5 = bf16[6,8192]{1,0:T(8,128)(2,1)S(1)} collective-permute-done((bf16[6,8192]{1,0:T(8,128)(2,1)S(1)}, bf16[6,8192]{1,0:T(8,128)(2,1)S(1)}, u32[]{:S(2)}, u32[]{:S(2)}) %collective-permute-start.5) | collective-permute-done | bytes 98336 | tf_op jit(solution)/shard_map/ppermute | solution.py:12
  55.3 0.0 collective-permute-start.6
  55.3 0.6 copy-done.2
  55.9 7.1 %collective-permute-done.6 = bf16[6,8192]{1,0:T(8,128)(2,1)} collective-permute-done((bf16[6,8192]{1,0:T(8,128)(2,1)S(1)}, bf16[6,8192]{1,0:T(8,128)(2,1)}, u32[]{:S(2)}, u32[]{:S(2)}) %collective-permute-start.6) | collective-permute-done | bytes 98336 | tf_op jit(solution)/shard_map/ppermute | solution.py:12
  63.0 5.6 %concatenate.3 = bf16[48,8192]{1,0:T(8,128)(2,1)S(1)} concatenate(bf16[6,8192]{1,0:T(8,128)(2,1)S(1)} %convert_element_type.11, bf16[6,8192]{1,0:T(8,128)(2,1)S(1)} %collective-permute-done, bf16[6,8192]{1,0:T(8,128)(2,1)S(1)} %collective-permute-done.1, bf16[6,8192]{1,0:T(8,128)(2,1)S(1)} %collective-permute-done.2, bf16[6,8192]{1,0:T(8,128)(2,1)S(1)} %collective-permute-done.3, ...), dimensions={0} | concatenate | bytes 1572864 | tf_op jit(solution)/shard_map/concatenate | solution.py:35
  68.7 0.8 %convolution_bitcast_fusion = f32[128,48]{0,1:T(8,128)S(1)} fusion(bf16[48,8192]{1,0:T(8,128)(2,1)S(1)} %concatenate.3, bf16[128,8192]{1,0:T(8,128)(2,1)S(1)} %copy-done), kind=kOutput, calls=%fused_computation.2 | convolution fusion | flops 100663296 | bytes 2908160 | tf_op jit(solution)/shard_map/dot_general | solution.py:36
  69.6 0.1 dynamic_update_slice.24
  69.7 0.1 dynamic_update_slice.25
  69.8 0.1 dynamic_update_slice.26
  70.0 0.1 dynamic_update_slice.27
  70.1 0.1 dynamic_update_slice.28
  70.2 0.1 dynamic_update_slice.29
  70.4 0.1 dynamic_update_slice.30
  70.5 0.1 dynamic_update_slice.31
  70.6 3.4 %psum.7 = f32[128,48]{0,1:T(8,128)S(1)} all-reduce(f32[128,48]{0,1:T(8,128)S(1)} %dynamic_update_slice.31), channel_id=1, replica_groups=mesh['grp'=2,'ex'=8,'dim'=2] {'dim'}, use_global_device_ids=true, to_apply=%region_0.1 | all-reduce | flops 6144 | bytes 49152 | tf_op jit(solution)/shard_map/psum | solution.py:64
  74.1 0.6 constant_dynamic-slice_fusion
  (9 shorter events, 0.1 us)
Async XLA Ops:
  0.0 68.7 %copy-start = (bf16[128,8192]{1,0:T(8,128)(2,1)S(1)}, bf16[128,8192]{1,0:T(8,128)(2,1)}, u32[]{:S(2)}) copy-start(bf16[128,8192]{1,0:T(8,128)(2,1)} %param.4) | copy-start | bytes 6291460
  0.0 2.9 %copy-start.3 = (bf16[6,8192]{1,0:T(8,128)(2,1)S(1)}, bf16[6,8192]{1,0:T(8,128)(2,1)}, u32[]{:S(2)}) copy-start(bf16[6,8192]{1,0:T(8,128)(2,1)} %param.3) | copy-start | bytes 294916
  5.6 9.5 %collective-permute-start = (bf16[6,8192]{1,0:T(8,128)(2,1)S(1)}, bf16[6,8192]{1,0:T(8,128)(2,1)S(1)}, u32[]{:S(2)}, u32[]{:S(2)}) collective-permute-start(bf16[6,8192]{1,0:T(8,128)(2,1)S(1)} %convert_element_type.11), channel_id=1, source_target_pairs={{14,0},{0,2},{2,4},{4,6},{6,8},{8,10},{10,12},{12,14},{15,1},{1,3}... | collective-permute-start | bytes 294920 | tf_op jit(solution)/shard_map/ppermute | solution.py:12
  15.1 7.7 %collective-permute-start.1 = (bf16[6,8192]{1,0:T(8,128)(2,1)S(1)}, bf16[6,8192]{1,0:T(8,128)(2,1)S(1)}, u32[]{:S(2)}, u32[]{:S(2)}) collective-permute-start(bf16[6,8192]{1,0:T(8,128)(2,1)S(1)} %collective-permute-done), channel_id=1, source_target_pairs={{14,0},{0,2},{2,4},{4,6},{6,8},{8,10},{10,12},{12,14},{15,1},{1,3}... | collective-permute-start | bytes 294920 | tf_op jit(solution)/shard_map/ppermute | solution.py:12
  22.8 7.7 %collective-permute-start.2 = (bf16[6,8192]{1,0:T(8,128)(2,1)S(1)}, bf16[6,8192]{1,0:T(8,128)(2,1)S(1)}, u32[]{:S(2)}, u32[]{:S(2)}) collective-permute-start(bf16[6,8192]{1,0:T(8,128)(2,1)S(1)} %collective-permute-done.1), channel_id=1, source_target_pairs={{14,0},{0,2},{2,4},{4,6},{6,8},{8,10},{10,12},{12,14},{15,1},{1,3}... | collective-permute-start | bytes 294920 | tf_op jit(solution)/shard_map/ppermute | solution.py:12
  30.5 7.7 %collective-permute-start.3 = (bf16[6,8192]{1,0:T(8,128)(2,1)S(1)}, bf16[6,8192]{1,0:T(8,128)(2,1)S(1)}, u32[]{:S(2)}, u32[]{:S(2)}) collective-permute-start(bf16[6,8192]{1,0:T(8,128)(2,1)S(1)} %collective-permute-done.2), channel_id=1, source_target_pairs={{14,0},{0,2},{2,4},{4,6},{6,8},{8,10},{10,12},{12,14},{15,1},{1,3}... | collective-permute-start | bytes 294920 | tf_op jit(solution)/shard_map/ppermute | solution.py:12
  38.1 7.7 %collective-permute-start.4 = (bf16[6,8192]{1,0:T(8,128)(2,1)S(1)}, bf16[6,8192]{1,0:T(8,128)(2,1)S(1)}, u32[]{:S(2)}, u32[]{:S(2)}) collective-permute-start(bf16[6,8192]{1,0:T(8,128)(2,1)S(1)} %collective-permute-done.3), channel_id=1, source_target_pairs={{14,0},{0,2},{2,4},{4,6},{6,8},{8,10},{10,12},{12,14},{15,1},{1,3}... | collective-permute-start | bytes 294920 | tf_op jit(solution)/shard_map/ppermute | solution.py:12
  45.8 0.6 copy-start.1
  46.4 8.8 %collective-permute-start.5 = (bf16[6,8192]{1,0:T(8,128)(2,1)S(1)}, bf16[6,8192]{1,0:T(8,128)(2,1)S(1)}, u32[]{:S(2)}, u32[]{:S(2)}) collective-permute-start(bf16[6,8192]{1,0:T(8,128)(2,1)S(1)} %collective-permute-done.4), channel_id=1, source_target_pairs={{14,0},{0,2},{2,4},{4,6},{6,8},{8,10},{10,12},{12,14},{15,1},{1,3}... | collective-permute-start | bytes 294920 | tf_op jit(solution)/shard_map/ppermute | solution.py:12
  55.3 0.7 copy-start.2
  55.3 7.8 %collective-permute-start.6 = (bf16[6,8192]{1,0:T(8,128)(2,1)S(1)}, bf16[6,8192]{1,0:T(8,128)(2,1)}, u32[]{:S(2)}, u32[]{:S(2)}) collective-permute-start(bf16[6,8192]{1,0:T(8,128)(2,1)S(1)} %collective-permute-done.5), channel_id=1, source_target_pairs={{14,0},{0,2},{2,4},{4,6},{6,8},{8,10},{10,12},{12,14},{15,1},{1,3}... | collective-permute-start | bytes 294920 | tf_op jit(solution)/shard_map/ppermute | solution.py:12
where the time goes:
time: 75.1 us; the launch traced here: 74.7 us
  waiting for transfers between devices  53.1 us (71%)
  local copies, waits for them, and re-layouts  11.9 us (16%)
  blocking collectives  3.42 us (5%)
  matrix products  3.07 us (4%)
  starting transfers between devices  3.02 us (4%)
    ppermute x7, waiting for transfers between devices, shifted(): return lax.ppermute(block, axis, route)  53.1 us
    concatenate x1, local copies, waits for them, and re-layouts, score_group(): joined = jnp.concatenate(held, 0)  5.64 us
    psum x1, blocking collectives, per_device(): summed = lax.psum(partial_value, 'dim')  3.42 us
    ppermute x7, starting transfers between devices, shifted(): return lax.ppermute(block, axis, route)  3.02 us
    reshape x1, local copies, waits for them, and re-layouts, per_device(): matrices = precond.reshape(dims_dev // block_size, block_size, block_size)  2.92 us
    dot_general x1, matrix products, per_device(): jnp.einsum('qbi,bij->qbj', grouped, matrices, preferred_element_type=jnp....  2.24 us
  transfers between devices with their start and end apart: 7, of which 7 were waited for; matrix products, arithmetic and copies ran while one was open for 0% of the time, Pallas kernels for 0%

commit v1 on v0

v1 whole, which is shorter than its diff:
```python
import math

import jax
import jax.numpy as jnp
from jax import lax
from jax.experimental import pallas as pl
from jax.experimental.pallas import tpu as pltpu
from jax.sharding import PartitionSpec as P

LANES = 256
FOLD = 8
CONTRACT_LAST = (((1,), (1,)), ((), ()))
VMEM_LIMIT = 40 * 1024 * 1024


def ring_scores(queries, train_grads, precond):
    cycle_size = lax.axis_size("ex")
    dim_size = lax.axis_size("dim")
    query_rows, dims_dev = queries.shape
    train_rows = train_grads.shape[0]
    block_size = precond.shape[1]
    all_queries = query_rows * cycle_size
    matrices = precond.reshape(dims_dev // block_size, block_size, block_size)
    grouped = queries.reshape(query_rows, dims_dev // block_size, block_size)
    own_rows = jnp.einsum("qbi,bij->qbj", grouped, matrices, preferred_element_type=jnp.float32)
    own_rows = own_rows.reshape(query_rows, dims_dev).astype(jnp.bfloat16)
    group_len = math.gcd(cycle_size, 8)
    my_index = lax.axis_index("ex")
    route = [(i, (i + 1) % cycle_size) for i in range(cycle_size)]

    def score_group(running, held, first_step):
        score_tile = lax.dot_general(
            train_grads, jnp.concatenate(held, 0), CONTRACT_LAST, preferred_element_type=jnp.float32
        )
        for offset in range(group_len):
            source = (my_index - first_step - offset) % cycle_size
            running = lax.dynamic_update_slice(
                running,
                score_tile[:, offset * query_rows : (offset + 1) * query_rows],
                (jnp.int32(0), source * query_rows),
            )
        return running

    moving = own_rows
    held = [moving]
    for _ in range(1, group_len):
        moving = lax.ppermute(moving, "ex", route)
        held.append(moving)
    running = jnp.zeros((train_rows, all_queries), jnp.float32)
    running = score_group(running, held, jnp.int32(0))

    def cycle_step(group, carry):
        moving, running = carry
        held = []
        for _ in range(group_len):
            moving = lax.ppermute(moving, "ex", route)
            held.append(moving)
        return (moving, score_group(running, held, (group * group_len).astype(jnp.int32)))

    moving, partial_value = lax.fori_loop(1, cycle_size // group_len, cycle_step, (moving, running))
    summed = lax.psum(partial_value, "dim")
    half_cols = all_queries // dim_size
    return lax.dynamic_slice_in_dim(summed, lax.axis_index("dim") * half_cols, half_cols, 1)


def fold_kernel(train_ref, precond_ref, folded_ref):
    train_rows, dims = train_ref.shape
    block = precond_ref.shape[0]
    row_block = lax.broadcasted_iota(jnp.int32, (LANES, LANES), 0) // block
    col_block = lax.broadcasted_iota(jnp.int32, (LANES, LANES), 1) // block
    diagonal = row_block == col_block
    for chunk in range(dims // LANES):
        at = pl.ds(chunk * LANES, LANES)
        stacked = jnp.concatenate([precond_ref[:, at]] * (LANES // block), 0)
        matrix = jnp.where(diagonal, stacked, jnp.zeros_like(stacked))
        value = jnp.dot(train_ref[:, at], matrix, preferred_element_type=jnp.float32)
        head = value.astype(jnp.bfloat16)
        folded_ref[0:train_rows, at] = head
        rest = value - head.astype(jnp.float32)
        folded_ref[train_rows : 2 * train_rows, at] = rest.astype(jnp.bfloat16)


def partial_scores(folded_ref, blocks):
    joined = jnp.concatenate(blocks, 0)
    rows, width = joined.shape
    part = lax.broadcasted_iota(jnp.int32, (rows, width), 0) % FOLD
    total = None
    for k in range(FOLD):
        masked = jnp.where(part == k, joined, jnp.zeros_like(joined))
        term = lax.dot_general(
            masked,
            folded_ref[:, k * width : (k + 1) * width],
            CONTRACT_LAST,
            preferred_element_type=jnp.float32,
        )
        total = term if total is None else total + term
    train_rows = total.shape[1] // 2
    total = total[:, :train_rows] + total[:, train_rows:]
    return total.reshape(rows // FOLD, FOLD, train_rows).sum(1)


def in_order(pieces, flip):
    placed = []
    for slot in range(len(pieces)):
        chosen = pieces[slot]
        for other in range(1, len(pieces)):
            chosen = jnp.where(flip == other, pieces[slot ^ other], chosen)
        placed.append(chosen)
    return jnp.concatenate(placed, 0)


def near_kernel(folded_ref, own_ref, x_ref, z_ref, xz_ref, far_ref, near_ref, first_ref):
    scores = partial_scores(folded_ref, [r[...] for r in (own_ref, x_ref, z_ref, xz_ref, far_ref)])
    count = scores.shape[0] // 5
    pieces = [scores[i * count : (i + 1) * count] for i in range(5)]
    near_ref[...] = in_order(pieces[:4], lax.rem(lax.axis_index("ex"), 4))
    first_ref[...] = pieces[4]


def far_kernel(folded_ref, x_ref, y_ref, xy_ref, near_ref, first_ref, keep_ref, send_ref):
    scores = partial_scores(folded_ref, [r[...] for r in (x_ref, y_ref, xy_ref)])
    count = scores.shape[0] // 3
    pieces = [first_ref[...]] + [scores[i * count : (i + 1) * count] for i in range(3)]
    place = lax.axis_index("ex")
    flip = lax.rem(place, 4)
    flip = jnp.where(lax.axis_index("grp") == 1, flip ^ 2, flip)
    far = in_order(pieces, flip)
    near = near_ref[...]
    near_stays = lax.axis_index("dim") == place // 4
    keep_ref[...] = jnp.where(near_stays, near, far)
    send_ref[...] = jnp.where(near_stays, far, near)


def call(kernel, outs, args, flops):
    vmem = pl.BlockSpec(memory_space=pltpu.VMEM)
    moved = sum(a.size * a.dtype.itemsize for a in args)
    return pl.pallas_call(
        kernel,
        out_shape=outs,
        in_specs=[vmem] * len(args),
        out_specs=jax.tree.map(lambda _: vmem, outs),
        compiler_params=pltpu.CompilerParams(vmem_limit_bytes=VMEM_LIMIT),
        cost_estimate=pl.CostEstimate(flops=flops, bytes_accessed=moved, transcendentals=0),
    )(*args)


def crossing_scores(queries, train_grads, precond):
    query_rows, dims = queries.shape
    train_rows = train_grads.shape[0]

    def swap(value, mask):
        return lax.ppermute(value, "ex", [(i, i ^ mask) for i in range(8)])

    def swap_both(value, place):
        route = [(g * 8 + e, place(g, e)) for g in range(2) for e in range(8)]
        return lax.ppermute(value, ("grp", "ex"), route)

    own = queries.reshape(query_rows * FOLD, dims // FOLD)
    far = swap_both(own, lambda g, e: g * 8 + (e ^ (6 if g else 4)))
    near_x = swap(own, 1)
    near_z = swap(own, 2)
    near_xz = swap(near_x, 2)
    far_x = swap(far, 1)
    far_xy = swap_both(far, lambda g, e: (1 - g) * 8 + (e ^ 1))
    far_y = lax.ppermute(far, "grp", [(0, 1), (1, 0)])

    folded = call(
        fold_kernel,
        jax.ShapeDtypeStruct((2 * train_rows, dims), jnp.bfloat16),
        (train_grads, precond.T),
        2 * train_rows * dims * LANES,
    )
    quarter = jax.ShapeDtypeStruct((query_rows, train_rows), jnp.float32)
    half = jax.ShapeDtypeStruct((query_rows * 4, train_rows), jnp.float32)
    flops = 4 * train_rows * dims * query_rows * FOLD
    near, first = call(
        near_kernel, (half, quarter), (folded, own, near_x, near_z, near_xz, far), 5 * flops
    )
    keep, send = call(
        far_kernel, (half, half), (folded, far_x, far_y, far_xy, near, first), 3 * flops
    )
    return (keep + lax.ppermute(send, "dim", [(0, 1), (1, 0)])).T


def solution(mesh):
    placed = (P("ex", "dim"), P(("grp", "ex"), "dim"), P("dim", None))
    crossing = mesh.shape["grp"] == 2 and mesh.shape["ex"] == 8 and mesh.shape["dim"] == 2
    return jax.shard_map(
        crossing_scores if crossing else ring_scores,
        mesh=mesh,
        in_specs=placed,
        out_specs=P(("grp", "ex"), "dim"),
        check_vma=False,
    )
```

time: 75.1 us -> 23.2 us (0.31)
  waiting for transfers between devices: 53.1 us -> 3.36 us
  starting transfers between devices: 3.02 us -> 11.4 us
  local copies, waits for them, and re-layouts: 11.9 us -> 3.88 us
  Pallas kernels: 0 us -> 3.72 us
  blocking collectives: 3.42 us -> 0 us
  matrix products: 3.07 us -> 0 us
    ppermute x7 -> x8, waiting for transfers between devices: 53.1 us -> 3.36 us  [the longest x2 2.18 us: swap_both(): return lax.ppermute(value, ('grp', 'ex'), route)]
    ppermute x7 -> x8, starting transfers between devices: 3.02 us -> 11.4 us  [the longest x4 5.57 us: swap(): return lax.ppermute(value, 'ex', [(i, i ^ mask) for i in range(8)])]
    concatenate x1 -> x0, local copies, waits for them, and re-layouts: 5.64 us -> none  [score_group(): joined = jnp.concatenate(held, 0)]
    pallas_call x0 -> x3, Pallas kernels: none -> 3.72 us  [call(): pl.pallas_call(kernel, out_shape=outs, in_specs=[vmem] * len(args), out_s...]
    psum x1 -> x0, blocking collectives: 3.42 us -> none  [per_device(): summed = lax.psum(partial_value, 'dim')]
    dot_general x2 -> x0, matrix products: 3.07 us -> none  [the longest x1 2.24 us: per_device(): jnp.einsum('qbi,bij->qbj', grouped, matrices, preferred_element_type=jnp....]
    reshape x2 -> x1, local copies, waits for them, and re-layouts: 3.1 us -> 1.07 us  [crossing_scores(): own = queries.reshape(query_rows * FOLD, dims // FOLD)]
    unnamed x8 -> x4, local copies, waits for them, and re-layouts: 1.3 us -> 2.81 us
  transfers between devices with their start and end apart: 7 -> 8, of which waited for: 7 -> 2; matrix products, arithmetic and copies ran while one was open for 0% -> 0% of each run, Pallas kernels for 0% -> 10%
where the time goes in v1:
time: 23.2 us; the launch traced here: 23 us
  starting transfers between devices  11.4 us (49%)
  local copies, waits for them, and re-layouts  3.88 us (17%)
  Pallas kernels  3.72 us (16%)
  waiting for transfers between devices  3.36 us (14%)
  other arithmetic  0.6 us (3%)
    ppermute x4, starting transfers between devices, swap(): return lax.ppermute(value, 'ex', [(i, i ^ mask) for i in range(8)])  5.57 us
    pallas_call x3, Pallas kernels, call(): pl.pallas_call(kernel, out_shape=outs, in_specs=[vmem] * len(args), out_s...  3.72 us
    ppermute x2, starting transfers between devices, swap_both(): return lax.ppermute(value, ('grp', 'ex'), route)  3.71 us
    unnamed x4, local copies, waits for them, and re-layouts  2.81 us
    ppermute x2, waiting for transfers between devices, swap_both(): return lax.ppermute(value, ('grp', 'ex'), route)  2.18 us
    ppermute x1, starting transfers between devices, crossing_scores(): far_y = lax.ppermute(far, 'grp', [(0, 1), (1, 0)])  2.04 us
    ppermute x1, waiting for transfers between devices, crossing_scores(): return (keep + lax.ppermute(send, 'dim', [(0, 1), (1, 0)])).T  1.16 us
    reshape x1, local copies, waits for them, and re-layouts, crossing_scores(): own = queries.reshape(query_rows * FOLD, dims // FOLD)  1.07 us
  transfers between devices with their start and end apart: 8, of which 2 were waited for; matrix products, arithmetic and copies ran while one was open for 0% of the time, Pallas kernels for 10%

profile of v1, /device:TPU:0, one launch (start us, length us, event | category | flops | bytes accessed | tf_op | source)
XLA Modules:
  0.0 23.0 jit_solution(2810395019600014308)
XLA Ops:
  0.0 1.1 %reshape.3.own_ref = bf16[48,1024]{1,0:T(8,128)(2,1)S(1)} reshape(bf16[6,8192]{1,0:T(8,128)(2,1)} %param.3) | data formatting | bytes 196608 | tf_op jit(solution)/shard_map/reshape | solution.py:158
  1.1 3.0 %collective-permute-start.4 = (bf16[48,1024]{1,0:T(8,128)(2,1)S(1)}, bf16[48,1024]{1,0:T(8,128)(2,1)S(1)}, u32[]{:S(2)}, u32[]{:S(2)}) collective-permute-start(bf16[48,1024]{1,0:T(8,128)(2,1)S(1)} %reshape.3.own_ref), channel_id=1, source_target_pairs={{0,2},{2,0},{4,6},{6,4},{8,10},{10,8},{12,14},{14,12},{1,3},{3,1},... | collective-permute-start | bytes 294920 | tf_op jit(solution)/shard_map/ppermute | solution.py:152
  4.1 2.6 %collective-permute-start = (bf16[48,1024]{1,0:T(8,128)(2,1)S(1)}, bf16[48,1024]{1,0:T(8,128)(2,1)S(1)}, u32[]{:S(2)}, u32[]{:S(2)}) collective-permute-start(bf16[48,1024]{1,0:T(8,128)(2,1)S(1)} %reshape.3.own_ref), channel_id=1, source_target_pairs={{0,8},{2,10},{4,12},{6,14},{8,0},{10,2},{12,4},{14,6},{16,28},{18,... | collective-permute-start | bytes 294920 | tf_op jit(solution)/shard_map/ppermute | solution.py:156
  6.7 1.6 %collective-permute-start.5 = (bf16[48,1024]{1,0:T(8,128)(2,1)S(1)}, bf16[48,1024]{1,0:T(8,128)(2,1)S(1)}, u32[]{:S(2)}, u32[]{:S(2)}) collective-permute-start(bf16[48,1024]{1,0:T(8,128)(2,1)S(1)} %reshape.3.own_ref), channel_id=1, source_target_pairs={{0,4},{2,6},{4,0},{6,2},{8,12},{10,14},{12,8},{14,10},{1,5},{3,7},... | collective-permute-start | bytes 294920 | tf_op jit(solution)/shard_map/ppermute | solution.py:152
  8.2 0.0 collective-permute-done.4.x_ref
  8.2 0.5 %collective-permute-start.6 = (bf16[48,1024]{1,0:T(8,128)(2,1)S(1)}, bf16[48,1024]{1,0:T(8,128)(2,1)S(1)}, u32[]{:S(2)}, u32[]{:S(2)}) collective-permute-start(bf16[48,1024]{1,0:T(8,128)(2,1)S(1)} %collective-permute-done.4.x_ref), channel_id=1, source_target_pairs={{0,4},{2,6},{4,0},{6,2},{8,12},{10,14},{12,8},{14,10},{1,5},{3,7},... | collective-permute-start | bytes 294920 | tf_op jit(solution)/shard_map/ppermute | solution.py:152
  8.8 2.2 %collective-permute-done.far_ref = bf16[48,1024]{1,0:T(8,128)(2,1)S(1)} collective-permute-done((bf16[48,1024]{1,0:T(8,128)(2,1)S(1)}, bf16[48,1024]{1,0:T(8,128)(2,1)S(1)}, u32[]{:S(2)}, u32[]{:S(2)}) %collective-permute-start) | collective-permute-done | bytes 98336 | tf_op jit(solution)/shard_map/ppermute | solution.py:156
  11.0 0.5 %collective-permute-start.1 = (bf16[48,1024]{1,0:T(8,128)(2,1)S(1)}, bf16[48,1024]{1,0:T(8,128)(2,1)S(1)}, u32[]{:S(2)}, u32[]{:S(2)}) collective-permute-start(bf16[48,1024]{1,0:T(8,128)(2,1)S(1)} %collective-permute-done.far_ref), channel_id=1, source_target_pairs={{0,2},{2,0},{4,6},{6,4},{8,10},{10,8},{12,14},{14,12},{1,3},{3,1},... | collective-permute-start | bytes 294920 | tf_op jit(solution)/shard_map/ppermute | solution.py:152
  11.4 2.0 %collective-permute-start.2 = (bf16[48,1024]{1,0:T(8,128)(2,1)S(1)}, bf16[48,1024]{1,0:T(8,128)(2,1)S(1)}, u32[]{:S(2)}, u32[]{:S(2)}) collective-permute-start(bf16[48,1024]{1,0:T(8,128)(2,1)S(1)} %collective-permute-done.far_ref), channel_id=1, source_target_pairs={{0,16},{16,0},{1,17},{17,1},{2,18},{18,2},{3,19},{19,3},{4,20},{20... | collective-permute-start | bytes 294920 | tf_op jit(solution)/shard_map/ppermute | solution.py:165
  13.5 1.1 %collective-permute-start.3 = (bf16[48,1024]{1,0:T(8,128)(2,1)S(1)}, bf16[48,1024]{1,0:T(8,128)(2,1)S(1)}, u32[]{:S(2)}, u32[]{:S(2)}) collective-permute-start(bf16[48,1024]{1,0:T(8,128)(2,1)S(1)} %collective-permute-done.far_ref), channel_id=1, source_target_pairs={{0,18},{2,16},{4,22},{6,20},{8,26},{10,24},{12,30},{14,28},{16,2},... | collective-permute-start | bytes 294920 | tf_op jit(solution)/shard_map/ppermute | solution.py:156
  14.6 0.0 copy-start
  14.6 1.6 %copy-done = bf16[128,8192]{1,0:T(8,128)(2,1)S(1)} copy-done((bf16[128,8192]{1,0:T(8,128)(2,1)S(1)}, bf16[128,8192]{1,0:T(8,128)(2,1)}, u32[]{:S(2)}) %copy-start) | copy-done | bytes 2097176
  16.2 0.0 copy-start.1
  16.2 1.2 %copy-done.1 = bf16[8192,64]{0,1:T(8,128)(2,1)S(1)} copy-done((bf16[8192,64]{0,1:T(8,128)(2,1)S(1)}, bf16[8192,64]{0,1:T(8,128)(2,1)}, u32[]{:S(2)}) %copy-start.1) | copy-done | bytes 1048600
  17.4 0.9 %shard_map.37.folded_ref = bf16[256,8192]{1,0:T(8,128)(2,1)S(1)} custom-call(bf16[128,8192]{1,0:T(8,128)(2,1)S(1)} %copy-done, bf16[64,8192]{1,0:T(8,128)(2,1)S(1)} %bitcast.3), custom_call_target="tpu_custom_call" | custom-call | flops 536870912 | bytes 3145728 | tf_op jit(solution)/shard_map/pallas_call | solution.py:137
  18.3 0.0 collective-permute-done.5.z_ref
  18.3 0.0 collective-permute-done.6.xz_ref
  18.3 1.3 %shard_map.38 = (f32[24,128]{1,0:T(8,128)S(1)}, f32[6,128]{1,0:T(8,128)S(1)}) custom-call(bf16[256,8192]{1,0:T(8,128)(2,1)S(1)} %shard_map.37.folded_ref, bf16[48,1024]{1,0:T(8,128)(2,1)S(1)} %reshape.3.own_ref, bf16[48,1024]{1,0:T(8,128)(2,1)S(1)} %collective-permute-done.4.x_ref, bf16[48,1024]{1,0:T(8,128)(2,1)S(1)} %collective-permute-done.5.z_ref, ...), custom_call_target="tpu_custom_call" | custom-call | flops 1006632960 | bytes 4685824 | tf_op jit(solution)/shard_map/pallas_call | solution.py:137
  19.6 0.0 collective-permute-done.1.x_ref
  19.6 0.0 collective-permute-done.2.y_ref
  19.6 0.0 collective-permute-done.3.xy_ref
  19.7 1.5 %shard_map.39 = (f32[24,128]{1,0:T(8,128)S(1)}, f32[24,128]{1,0:T(8,128)S(1)}) custom-call(bf16[256,8192]{1,0:T(8,128)(2,1)S(1)} %shard_map.37.folded_ref, bf16[48,1024]{1,0:T(8,128)(2,1)S(1)} %collective-permute-done.1.x_ref, bf16[48,1024]{1,0:T(8,128)(2,1)S(1)} %collective-permute-done.2.y_ref, bf16[48,1024]{1,0:T(8,128)(2,1)S(1)} %collective-permute-done.3.xy_ref, ...), custom_call_target="tpu_custom_call" | custom-call | flops 603979776 | bytes 4504576 | tf_op jit(solution)/shard_map/pallas_call | solution.py:137
  21.2 0.1 collective-permute-start.7
  21.3 1.2 %collective-permute-done.7 = f32[24,128]{1,0:T(8,128)S(1)} collective-permute-done((f32[24,128]{1,0:T(8,128)S(1)}, f32[24,128]{1,0:T(8,128)S(1)}, u32[]{:S(2)}, u32[]{:S(2)}) %collective-permute-start.7) | collective-permute-done | bytes 12320 | tf_op jit(solution)/shard_map/ppermute | solution.py:182
  22.4 0.6 %add_bitcast_fusion = f32[128,24]{0,1:T(8,128)} fusion(f32[24,128]{1,0:T(8,128)S(1)} %get-tuple-element.11, f32[24,128]{1,0:T(8,128)S(1)} %collective-permute-done.7), kind=kLoop, calls=%fused_computation | loop fusion | flops 3072 | bytes 36864 | tf_op jit(solution)/shard_map/transpose | solution.py:182
Async XLA Ops:
  1.1 7.2 %collective-permute-start.4 = (bf16[48,1024]{1,0:T(8,128)(2,1)S(1)}, bf16[48,1024]{1,0:T(8,128)(2,1)S(1)}, u32[]{:S(2)}, u32[]{:S(2)}) collective-permute-start(bf16[48,1024]{1,0:T(8,128)(2,1)S(1)} %reshape.3.own_ref), channel_id=1, source_target_pairs={{0,2},{2,0},{4,6},{6,4},{8,10},{10,8},{12,14},{14,12},{1,3},{3,1},... | collective-permute-start | bytes 294920 | tf_op jit(solution)/shard_map/ppermute | solution.py:152
  4.1 6.9 %collective-permute-start = (bf16[48,1024]{1,0:T(8,128)(2,1)S(1)}, bf16[48,1024]{1,0:T(8,128)(2,1)S(1)}, u32[]{:S(2)}, u32[]{:S(2)}) collective-permute-start(bf16[48,1024]{1,0:T(8,128)(2,1)S(1)} %reshape.3.own_ref), channel_id=1, source_target_pairs={{0,8},{2,10},{4,12},{6,14},{8,0},{10,2},{12,4},{14,6},{16,28},{18,... | collective-permute-start | bytes 294920 | tf_op jit(solution)/shard_map/ppermute | solution.py:156
  6.7 11.6 %collective-permute-start.5 = (bf16[48,1024]{1,0:T(8,128)(2,1)S(1)}, bf16[48,1024]{1,0:T(8,128)(2,1)S(1)}, u32[]{:S(2)}, u32[]{:S(2)}) collective-permute-start(bf16[48,1024]{1,0:T(8,128)(2,1)S(1)} %reshape.3.own_ref), channel_id=1, source_target_pairs={{0,4},{2,6},{4,0},{6,2},{8,12},{10,14},{12,8},{14,10},{1,5},{3,7},... | collective-permute-start | bytes 294920 | tf_op jit(solution)/shard_map/ppermute | solution.py:152
  8.2 10.1 %collective-permute-start.6 = (bf16[48,1024]{1,0:T(8,128)(2,1)S(1)}, bf16[48,1024]{1,0:T(8,128)(2,1)S(1)}, u32[]{:S(2)}, u32[]{:S(2)}) collective-permute-start(bf16[48,1024]{1,0:T(8,128)(2,1)S(1)} %collective-permute-done.4.x_ref), channel_id=1, source_target_pairs={{0,4},{2,6},{4,0},{6,2},{8,12},{10,14},{12,8},{14,10},{1,5},{3,7},... | collective-permute-start | bytes 294920 | tf_op jit(solution)/shard_map/ppermute | solution.py:152
  11.0 8.7 %collective-permute-start.1 = (bf16[48,1024]{1,0:T(8,128)(2,1)S(1)}, bf16[48,1024]{1,0:T(8,128)(2,1)S(1)}, u32[]{:S(2)}, u32[]{:S(2)}) collective-permute-start(bf16[48,1024]{1,0:T(8,128)(2,1)S(1)} %collective-permute-done.far_ref), channel_id=1, source_target_pairs={{0,2},{2,0},{4,6},{6,4},{8,10},{10,8},{12,14},{14,12},{1,3},{3,1},... | collective-permute-start | bytes 294920 | tf_op jit(solution)/shard_map/ppermute | solution.py:152
  11.4 8.2 %collective-permute-start.2 = (bf16[48,1024]{1,0:T(8,128)(2,1)S(1)}, bf16[48,1024]{1,0:T(8,128)(2,1)S(1)}, u32[]{:S(2)}, u32[]{:S(2)}) collective-permute-start(bf16[48,1024]{1,0:T(8,128)(2,1)S(1)} %collective-permute-done.far_ref), channel_id=1, source_target_pairs={{0,16},{16,0},{1,17},{17,1},{2,18},{18,2},{3,19},{19,3},{4,20},{20... | collective-permute-start | bytes 294920 | tf_op jit(solution)/shard_map/ppermute | solution.py:165
  13.5 6.2 %collective-permute-start.3 = (bf16[48,1024]{1,0:T(8,128)(2,1)S(1)}, bf16[48,1024]{1,0:T(8,128)(2,1)S(1)}, u32[]{:S(2)}, u32[]{:S(2)}) collective-permute-start(bf16[48,1024]{1,0:T(8,128)(2,1)S(1)} %collective-permute-done.far_ref), channel_id=1, source_target_pairs={{0,18},{2,16},{4,22},{6,20},{8,26},{10,24},{12,30},{14,28},{16,2},... | collective-permute-start | bytes 294920 | tf_op jit(solution)/shard_map/ppermute | solution.py:156
  14.6 1.6 %copy-start = (bf16[128,8192]{1,0:T(8,128)(2,1)S(1)}, bf16[128,8192]{1,0:T(8,128)(2,1)}, u32[]{:S(2)}) copy-start(bf16[128,8192]{1,0:T(8,128)(2,1)} %train_ref.1) | copy-start | bytes 6291460
  16.2 1.2 %copy-start.1 = (bf16[8192,64]{0,1:T(8,128)(2,1)S(1)}, bf16[8192,64]{0,1:T(8,128)(2,1)}, u32[]{:S(2)}) copy-start(bf16[8192,64]{0,1:T(8,128)(2,1)} %param.5) | copy-start | bytes 3145732
  21.2 1.2 %collective-permute-start.7 = (f32[24,128]{1,0:T(8,128)S(1)}, f32[24,128]{1,0:T(8,128)S(1)}, u32[]{:S(2)}, u32[]{:S(2)}) collective-permute-start(f32[24,128]{1,0:T(8,128)S(1)} %get-tuple-element.12), channel_id=1, source_target_pairs={{0,1},{1,0},{2,3},{3,2},{4,5},{5,4},{6,7},{7,6},{8,9},{9,8},{10,11... | collective-permute-start | bytes 36872 | tf_op jit(solution)/shard_map/ppermute | solution.py:182

commit v2 on v1

--- a/solution.py
+++ b/solution.py
@@ -8,7 +8,7 @@
 from jax.sharding import PartitionSpec as P
 
 LANES = 256
-FOLD = 8
+PACKED = 8
 CONTRACT_LAST = (((1,), (1,)), ((), ()))
 VMEM_LIMIT = 40 * 1024 * 1024
 
@@ -80,23 +80,50 @@
         folded_ref[train_rows : 2 * train_rows, at] = rest.astype(jnp.bfloat16)
 
 
-def partial_scores(folded_ref, blocks):
-    joined = jnp.concatenate(blocks, 0)
-    rows, width = joined.shape
-    part = lax.broadcasted_iota(jnp.int32, (rows, width), 0) % FOLD
-    total = None
-    for k in range(FOLD):
-        masked = jnp.where(part == k, joined, jnp.zeros_like(joined))
-        term = lax.dot_general(
-            masked,
-            folded_ref[:, k * width : (k + 1) * width],
-            CONTRACT_LAST,
-            preferred_element_type=jnp.float32,
-        )
-        total = term if total is None else total + term
-    train_rows = total.shape[1] // 2
-    total = total[:, :train_rows] + total[:, train_rows:]
-    return total.reshape(rows // FOLD, FOLD, train_rows).sum(1)
+def pack_kernel(queries_ref, packed_ref):
+    rows, dims = queries_ref.shape
+    width = packed_ref.shape[1]
+    each = width // (dims - width)
+    main = queries_ref[:, :width].astype(jnp.float32)
+    tail = queries_ref[:, width:].astype(jnp.float32)
+    below = jnp.concatenate(
+        [jnp.concatenate([tail[i : i + 1] for i in range(m, rows, each)], 0) for m in range(each)],
+        1,
+    )
+    packed_ref[...] = jnp.concatenate([main, below], 0).astype(jnp.bfloat16)
+
+
+def partial_scores(folded_ref, refs):
+    width = refs[0].shape[1]
+    dims = folded_ref.shape[1]
+    tail = dims - width
+    each = width // tail
+    rows = width * PACKED // dims
+    joined = jnp.concatenate([r[...].astype(jnp.float32) for r in refs], 0)
+    tails = jnp.concatenate([joined[:, m * tail : (m + 1) * tail] for m in range(each)], 0)
+    main = lax.dot_general(
+        joined.astype(jnp.bfloat16),
+        folded_ref[:, :width],
+        CONTRACT_LAST,
+        preferred_element_type=jnp.float32,
+    )
+    rest = lax.dot_general(
+        tails.astype(jnp.bfloat16),
+        folded_ref[:, width:],
+        CONTRACT_LAST,
+        preferred_element_type=jnp.float32,
+    )
+    train_rows = main.shape[1] // 2
+    main = main[:, :train_rows] + main[:, train_rows:]
+    rest = rest[:, :train_rows] + rest[:, train_rows:]
+    scores = []
+    for i in range(len(refs)):
+        below = []
+        for row in range(rows):
+            at = (row % each * len(refs) + i) * PACKED + rows + row // each
+            below.append(rest[at : at + 1])
+        scores.append(main[i * PACKED : i * PACKED + rows] + jnp.concatenate(below, 0))
+    return scores
 
 
 def in_order(pieces, flip):
@@ -109,21 +136,17 @@
     return jnp.concatenate(placed, 0)
 
 
-def near_kernel(folded_ref, own_ref, x_ref, z_ref, xz_ref, far_ref, near_ref, first_ref):
-    scores = partial_scores(folded_ref, [r[...] for r in (own_ref, x_ref, z_ref, xz_ref, far_ref)])
-    count = scores.shape[0] // 5
-    pieces = [scores[i * count : (i + 1) * count] for i in range(5)]
+def near_kernel(folded_ref, own_ref, xz_ref, z_ref, x_ref, far_ref, near_ref, first_ref):
+    pieces = partial_scores(folded_ref, (own_ref, x_ref, z_ref, xz_ref, far_ref))
     near_ref[...] = in_order(pieces[:4], lax.rem(lax.axis_index("ex"), 4))
     first_ref[...] = pieces[4]
 
 
-def far_kernel(folded_ref, x_ref, y_ref, xy_ref, near_ref, first_ref, keep_ref, send_ref):
-    scores = partial_scores(folded_ref, [r[...] for r in (x_ref, y_ref, xy_ref)])
-    count = scores.shape[0] // 3
-    pieces = [first_ref[...]] + [scores[i * count : (i + 1) * count] for i in range(3)]
+def far_kernel(folded_ref, x_ref, z_ref, y_ref, near_ref, first_ref, keep_ref, send_ref):
+    pieces = [first_ref[...]] + partial_scores(folded_ref, (x_ref, z_ref, y_ref))
     place = lax.axis_index("ex")
     flip = lax.rem(place, 4)
-    flip = jnp.where(lax.axis_index("grp") == 1, flip ^ 2, flip)
+    flip = flip ^ jnp.where(lax.axis_index("grp") == 1, 2, 1)
     far = in_order(pieces, flip)
     near = near_ref[...]
     near_stays = lax.axis_index("dim") == place // 4
@@ -155,30 +178,33 @@
         route = [(g * 8 + e, place(g, e)) for g in range(2) for e in range(8)]
         return lax.ppermute(value, ("grp", "ex"), route)
 
-    own = queries.reshape(query_rows * FOLD, dims // FOLD)
-    far = swap_both(own, lambda g, e: g * 8 + (e ^ (6 if g else 4)))
-    near_x = swap(own, 1)
-    near_z = swap(own, 2)
-    near_xz = swap(near_x, 2)
-    far_x = swap(far, 1)
-    far_xy = swap_both(far, lambda g, e: (1 - g) * 8 + (e ^ 1))
-    far_y = lax.ppermute(far, "grp", [(0, 1), (1, 0)])
-
+    own = call(
+        pack_kernel,
+        jax.ShapeDtypeStruct((PACKED, query_rows * dims // PACKED), jnp.bfloat16),
+        (queries,),
+        5_000_000_000,
+    )
+    far = swap_both(own, lambda g, e: g * 8 + (e ^ (6 if g else 5)))
     folded = call(
         fold_kernel,
         jax.ShapeDtypeStruct((2 * train_rows, dims), jnp.bfloat16),
         (train_grads, precond.T),
         2 * train_rows * dims * LANES,
     )
+    far, folded = lax.optimization_barrier((far, folded))
+    far_x = swap(far, 1)
+    far_z = swap(far, 2)
+    far_y = lax.ppermute(far, "grp", [(0, 1), (1, 0)])
+    near_x = swap(own, 1)
+    near_z = swap(own, 2)
+    near_xz = swap(own, 3)
     quarter = jax.ShapeDtypeStruct((query_rows, train_rows), jnp.float32)
     half = jax.ShapeDtypeStruct((query_rows * 4, train_rows), jnp.float32)
-    flops = 4 * train_rows * dims * query_rows * FOLD
+    flops = 4 * train_rows * dims * LANES
     near, first = call(
-        near_kernel, (half, quarter), (folded, own, near_x, near_z, near_xz, far), 5 * flops
-    )
-    keep, send = call(
-        far_kernel, (half, half), (folded, far_x, far_y, far_xy, near, first), 3 * flops
-    )
+        near_kernel, (half, quarter), (folded, own, near_xz, near_z, near_x, far), flops
+    )
+    keep, send = call(far_kernel, (half, half), (folded, far_x, far_z, far_y, near, first), flops)
     return (keep + lax.ppermute(send, "dim", [(0, 1), (1, 0)])).T
 
 

time: 23.2 us -> 20.3 us (0.88)
  local copies, waits for them, and re-layouts: 3.88 us -> 1 us
    unnamed x4 -> x6, local copies, waits for them, and re-layouts: 2.81 us -> 1 us
    ppermute x4 -> x5, waiting for transfers between devices: 0.01 us -> 1.71 us  [swap(): return lax.ppermute(value, 'ex', [(i, i ^ mask) for i in range(8)])]
    ppermute x2 -> x1, waiting for transfers between devices: 2.18 us -> 0.6 us  [swap_both(): return lax.ppermute(value, ('grp', 'ex'), route)]
    ppermute x2 -> x1, starting transfers between devices: 3.71 us -> 5.03 us  [swap_both(): return lax.ppermute(value, ('grp', 'ex'), route)]
    reshape x1 -> x0, local copies, waits for them, and re-layouts: 1.07 us -> none  [crossing_scores(): own = queries.reshape(query_rows * FOLD, dims // FOLD)]
    ppermute x1, starting transfers between devices: 2.04 us -> 1.07 us  [crossing_scores(): far_y = lax.ppermute(far, 'grp', [(0, 1), (1, 0)])]
    ppermute x4 -> x5, starting transfers between devices: 5.57 us -> 5.11 us  [swap(): return lax.ppermute(value, 'ex', [(i, i ^ mask) for i in range(8)])]
    pallas_call x3 -> x4, Pallas kernels: 3.72 us -> 3.73 us  [call(): pl.pallas_call(kernel, out_shape=outs, in_specs=[vmem] * len(args), out_s...]
  transfers between devices with their start and end apart: 8 -> 8, of which waited for: 2 -> 5; matrix products, arithmetic and copies ran while one was open for 0% -> 0% of each run, Pallas kernels for 10% -> 12%
where the time goes in v2:
time: 20.3 us; the launch traced here: 20.1 us
  starting transfers between devices  11.3 us (56%)
  Pallas kernels  3.73 us (18%)
  waiting for transfers between devices  3.48 us (17%)
  local copies, waits for them, and re-layouts  1 us (5%)
  other arithmetic  0.6 us (3%)
    ppermute x5, starting transfers between devices, swap(): return lax.ppermute(value, 'ex', [(i, i ^ mask) for i in range(8)])  5.11 us
    ppermute x1, starting transfers between devices, swap_both(): return lax.ppermute(value, ('grp', 'ex'), route)  5.03 us
    pallas_call x4, Pallas kernels, call(): pl.pallas_call(kernel, out_shape=outs, in_specs=[vmem] * len(args), out_s...  3.73 us
    ppermute x5, waiting for transfers between devices, swap(): return lax.ppermute(value, 'ex', [(i, i ^ mask) for i in range(8)])  1.71 us
    ppermute x1, waiting for transfers between devices, crossing_scores(): return (keep + lax.ppermute(send, 'dim', [(0, 1), (1, 0)])).T  1.16 us
    ppermute x1, starting transfers between devices, crossing_scores(): far_y = lax.ppermute(far, 'grp', [(0, 1), (1, 0)])  1.07 us
    unnamed x6, local copies, waits for them, and re-layouts  1 us
    ppermute x1, waiting for transfers between devices, swap_both(): return lax.ppermute(value, ('grp', 'ex'), route)  0.6 us
  transfers between devices with their start and end apart: 8, of which 5 were waited for; matrix products, arithmetic and copies ran while one was open for 0% of the time, Pallas kernels for 12%

profile of v2, /device:TPU:0, one launch (start us, length us, event | category | flops | bytes accessed | tf_op | source)
XLA Modules:
  0.0 20.1 jit_solution(16729903217554528772)
XLA Ops:
  0.0 0.0 copy-start.1
  0.0 0.0 copy-start.2
  0.0 1.0 %copy-done.2 = bf16[6,8192]{1,0:T(8,128)(2,1)S(1)} copy-done((bf16[6,8192]{1,0:T(8,128)(2,1)S(1)}, bf16[6,8192]{1,0:T(8,128)(2,1)}, u32[]{:S(2)}) %copy-start.2) | copy-done | bytes 98328
  1.0 0.0 copy-start
  1.0 5.0 %collective-permute-start = (bf16[8,6144]{1,0:T(8,128)(2,1)S(1)}, bf16[8,6144]{1,0:T(8,128)(2,1)S(1)}, u32[]{:S(2)}, u32[]{:S(2)}) collective-permute-start(bf16[8,6144]{1,0:T(8,128)(2,1)S(1)} %shard_map.37.own_ref), channel_id=1, source_target_pairs={{0,10},{2,8},{4,14},{6,12},{8,2},{10,0},{12,6},{14,4},{16,28},{18,... | collective-permute-start | bytes 294920 | tf_op jit(solution)/shard_map/ppermute | solution.py:179
  6.1 0.5 %collective-permute-start.6 = (bf16[8,6144]{1,0:T(8,128)(2,1)S(1)}, bf16[8,6144]{1,0:T(8,128)(2,1)S(1)}, u32[]{:S(2)}, u32[]{:S(2)}) collective-permute-start(bf16[8,6144]{1,0:T(8,128)(2,1)S(1)} %shard_map.37.own_ref), channel_id=1, source_target_pairs={{0,2},{2,0},{4,6},{6,4},{8,10},{10,8},{12,14},{14,12},{1,3},{3,1},... | collective-permute-start | bytes 294920 | tf_op jit(solution)/shard_map/ppermute | solution.py:175
  6.6 1.6 %collective-permute-start.5 = (bf16[8,6144]{1,0:T(8,128)(2,1)S(1)}, bf16[8,6144]{1,0:T(8,128)(2,1)S(1)}, u32[]{:S(2)}, u32[]{:S(2)}) collective-permute-start(bf16[8,6144]{1,0:T(8,128)(2,1)S(1)} %shard_map.37.own_ref), channel_id=1, source_target_pairs={{0,4},{2,6},{4,0},{6,2},{8,12},{10,14},{12,8},{14,10},{1,5},{3,7},... | collective-permute-start | bytes 294920 | tf_op jit(solution)/shard_map/ppermute | solution.py:175
  8.2 1.4 %collective-permute-start.4 = (bf16[8,6144]{1,0:T(8,128)(2,1)S(1)}, bf16[8,6144]{1,0:T(8,128)(2,1)S(1)}, u32[]{:S(2)}, u32[]{:S(2)}) collective-permute-start(bf16[8,6144]{1,0:T(8,128)(2,1)S(1)} %shard_map.37.own_ref), channel_id=1, source_target_pairs={{0,6},{2,4},{4,2},{6,0},{8,14},{10,12},{12,10},{14,8},{1,7},{3,5},... | collective-permute-start | bytes 294920 | tf_op jit(solution)/shard_map/ppermute | solution.py:175
  9.6 0.0 copy-done.1
  9.6 0.0 copy-done
  9.6 0.9 %shard_map.38.folded_ref = bf16[256,8192]{1,0:T(8,128)(2,1)S(1)} custom-call(bf16[128,8192]{1,0:T(8,128)(2,1)S(1)} %copy-done, bf16[64,8192]{1,0:T(8,128)(2,1)S(1)} %bitcast.3), custom_call_target="tpu_custom_call" | custom-call | flops 536870912 | bytes 3145728 | tf_op jit(solution)/shard_map/pallas_call | solution.py:160
  10.5 0.6 %collective-permute-done.far_ref = bf16[8,6144]{1,0:T(8,128)(2,1)S(1)} collective-permute-done((bf16[8,6144]{1,0:T(8,128)(2,1)S(1)}, bf16[8,6144]{1,0:T(8,128)(2,1)S(1)}, u32[]{:S(2)}, u32[]{:S(2)}) %collective-permute-start) | collective-permute-done | bytes 98336 | tf_op jit(solution)/shard_map/ppermute | solution.py:179
  11.1 1.1 %collective-permute-start.3 = (bf16[8,6144]{1,0:T(8,128)(2,1)S(1)}, bf16[8,6144]{1,0:T(8,128)(2,1)S(1)}, u32[]{:S(2)}, u32[]{:S(2)}) collective-permute-start(bf16[8,6144]{1,0:T(8,128)(2,1)S(1)} %collective-permute-done.far_ref), channel_id=1, source_target_pairs={{0,16},{16,0},{1,17},{17,1},{2,18},{18,2},{3,19},{19,3},{4,20},{20... | collective-permute-start | bytes 294920 | tf_op jit(solution)/shard_map/ppermute | solution.py:197
  12.2 0.1 collective-permute-start.2
  12.3 0.0 collective-permute-done.6.x_ref
  12.3 1.5 %collective-permute-start.1 = (bf16[8,6144]{1,0:T(8,128)(2,1)S(1)}, bf16[8,6144]{1,0:T(8,128)(2,1)S(1)}, u32[]{:S(2)}, u32[]{:S(2)}) collective-permute-start(bf16[8,6144]{1,0:T(8,128)(2,1)S(1)} %collective-permute-done.far_ref), channel_id=1, source_target_pairs={{0,2},{2,0},{4,6},{6,4},{8,10},{10,8},{12,14},{14,12},{1,3},{3,1},... | collective-permute-start | bytes 294920 | tf_op jit(solution)/shard_map/ppermute | solution.py:175
  13.8 0.0 collective-permute-done.5.z_ref
  13.8 1.0 %collective-permute-done.4.xz_ref = bf16[8,6144]{1,0:T(8,128)(2,1)S(1)} collective-permute-done((bf16[8,6144]{1,0:T(8,128)(2,1)S(1)}, bf16[8,6144]{1,0:T(8,128)(2,1)S(1)}, u32[]{:S(2)}, u32[]{:S(2)}) %collective-permute-start.4) | collective-permute-done | bytes 98336 | tf_op jit(solution)/shard_map/ppermute | solution.py:175
  14.8 1.4 %shard_map.39 = (f32[24,128]{1,0:T(8,128)S(1)}, f32[6,128]{1,0:T(8,128)S(1)}) custom-call(bf16[256,8192]{1,0:T(8,128)(2,1)S(1)} %shard_map.38.folded_ref, bf16[8,6144]{1,0:T(8,128)(2,1)S(1)} %shard_map.37.own_ref, bf16[8,6144]{1,0:T(8,128)(2,1)S(1)} %collective-permute-done.4.xz_ref, bf16[8,6144]{1,0:T(8,128)(2,1)S(1)} %collective-permute-done.5.z_ref, ...), custom_call_target="tpu_custom_call" | custom-call | flops 1073741824 | bytes 4685824 | tf_op jit(solution)/shard_map/pallas_call | solution.py:160
  16.2 0.0 collective-permute-done.3.y_ref
  16.2 0.6 %collective-permute-done.2.z_ref = bf16[8,6144]{1,0:T(8,128)(2,1)S(1)} collective-permute-done((bf16[8,6144]{1,0:T(8,128)(2,1)S(1)}, bf16[8,6144]{1,0:T(8,128)(2,1)S(1)}, u32[]{:S(2)}, u32[]{:S(2)}) %collective-permute-start.2) | collective-permute-done | bytes 98336 | tf_op jit(solution)/shard_map/ppermute | solution.py:175
  16.8 0.1 collective-permute-done.1.x_ref
  16.9 1.4 %shard_map.40 = (f32[24,128]{1,0:T(8,128)S(1)}, f32[24,128]{1,0:T(8,128)S(1)}) custom-call(bf16[256,8192]{1,0:T(8,128)(2,1)S(1)} %shard_map.38.folded_ref, bf16[8,6144]{1,0:T(8,128)(2,1)S(1)} %collective-permute-done.1.x_ref, bf16[8,6144]{1,0:T(8,128)(2,1)S(1)} %collective-permute-done.2.z_ref, bf16[8,6144]{1,0:T(8,128)(2,1)S(1)} %collective-permute-done.3.y_ref, ...), custom_call_target="tpu_custom_call" | custom-call | flops 1073741824 | bytes 4504576 | tf_op jit(solution)/shard_map/pallas_call | solution.py:160
  18.3 0.1 collective-permute-start.7
  18.4 1.2 %collective-permute-done.7 = f32[24,128]{1,0:T(8,128)S(1)} collective-permute-done((f32[24,128]{1,0:T(8,128)S(1)}, f32[24,128]{1,0:T(8,128)S(1)}, u32[]{:S(2)}, u32[]{:S(2)}) %collective-permute-start.7) | collective-permute-done | bytes 12320 | tf_op jit(solution)/shard_map/ppermute | solution.py:208
  19.5 0.6 %add_bitcast_fusion = f32[128,24]{0,1:T(8,128)} fusion(f32[24,128]{1,0:T(8,128)S(1)} %get-tuple-element.15, f32[24,128]{1,0:T(8,128)S(1)} %collective-permute-done.7), kind=kLoop, calls=%fused_computation | loop fusion | flops 3072 | bytes 36864 | tf_op jit(solution)/shard_map/transpose | solution.py:208
  (1 shorter events, 0.0 us)
Async XLA Ops:
  0.0 9.6 %copy-start.1 = (bf16[8192,64]{0,1:T(8,128)(2,1)S(1)}, bf16[8192,64]{0,1:T(8,128)(2,1)}, u32[]{:S(2)}) copy-start(bf16[8192,64]{0,1:T(8,128)(2,1)} %param.5) | copy-start | bytes 3145732
  0.0 1.0 %copy-start.2 = (bf16[6,8192]{1,0:T(8,128)(2,1)S(1)}, bf16[6,8192]{1,0:T(8,128)(2,1)}, u32[]{:S(2)}) copy-start(bf16[6,8192]{1,0:T(8,128)(2,1)} %queries_ref.1) | copy-start | bytes 294916
  1.0 8.6 %copy-start = (bf16[128,8192]{1,0:T(8,128)(2,1)S(1)}, bf16[128,8192]{1,0:T(8,128)(2,1)}, u32[]{:S(2)}) copy-start(bf16[128,8192]{1,0:T(8,128)(2,1)} %train_ref.1) | copy-start | bytes 6291460
  1.0 10.0 %collective-permute-start = (bf16[8,6144]{1,0:T(8,128)(2,1)S(1)}, bf16[8,6144]{1,0:T(8,128)(2,1)S(1)}, u32[]{:S(2)}, u32[]{:S(2)}) collective-permute-start(bf16[8,6144]{1,0:T(8,128)(2,1)S(1)} %shard_map.37.own_ref), channel_id=1, source_target_pairs={{0,10},{2,8},{4,14},{6,12},{8,2},{10,0},{12,6},{14,4},{16,28},{18,... | collective-permute-start | bytes 294920 | tf_op jit(solution)/shard_map/ppermute | solution.py:179
  6.1 6.2 %collective-permute-start.6 = (bf16[8,6144]{1,0:T(8,128)(2,1)S(1)}, bf16[8,6144]{1,0:T(8,128)(2,1)S(1)}, u32[]{:S(2)}, u32[]{:S(2)}) collective-permute-start(bf16[8,6144]{1,0:T(8,128)(2,1)S(1)} %shard_map.37.own_ref), channel_id=1, source_target_pairs={{0,2},{2,0},{4,6},{6,4},{8,10},{10,8},{12,14},{14,12},{1,3},{3,1},... | collective-permute-start | bytes 294920 | tf_op jit(solution)/shard_map/ppermute | solution.py:175
  6.6 7.2 %collective-permute-start.5 = (bf16[8,6144]{1,0:T(8,128)(2,1)S(1)}, bf16[8,6144]{1,0:T(8,128)(2,1)S(1)}, u32[]{:S(2)}, u32[]{:S(2)}) collective-permute-start(bf16[8,6144]{1,0:T(8,128)(2,1)S(1)} %shard_map.37.own_ref), channel_id=1, source_target_pairs={{0,4},{2,6},{4,0},{6,2},{8,12},{10,14},{12,8},{14,10},{1,5},{3,7},... | collective-permute-start | bytes 294920 | tf_op jit(solution)/shard_map/ppermute | solution.py:175
  8.2 6.6 %collective-permute-start.4 = (bf16[8,6144]{1,0:T(8,128)(2,1)S(1)}, bf16[8,6144]{1,0:T(8,128)(2,1)S(1)}, u32[]{:S(2)}, u32[]{:S(2)}) collective-permute-start(bf16[8,6144]{1,0:T(8,128)(2,1)S(1)} %shard_map.37.own_ref), channel_id=1, source_target_pairs={{0,6},{2,4},{4,2},{6,0},{8,14},{10,12},{12,10},{14,8},{1,7},{3,5},... | collective-permute-start | bytes 294920 | tf_op jit(solution)/shard_map/ppermute | solution.py:175
  11.1 5.1 %collective-permute-start.3 = (bf16[8,6144]{1,0:T(8,128)(2,1)S(1)}, bf16[8,6144]{1,0:T(8,128)(2,1)S(1)}, u32[]{:S(2)}, u32[]{:S(2)}) collective-permute-start(bf16[8,6144]{1,0:T(8,128)(2,1)S(1)} %collective-permute-done.far_ref), channel_id=1, source_target_pairs={{0,16},{16,0},{1,17},{17,1},{2,18},{18,2},{3,19},{19,3},{4,20},{20... | collective-permute-start | bytes 294920 | tf_op jit(solution)/shard_map/ppermute | solution.py:197
  12.2 4.6 %collective-permute-start.2 = (bf16[8,6144]{1,0:T(8,128)(2,1)S(1)}, bf16[8,6144]{1,0:T(8,128)(2,1)S(1)}, u32[]{:S(2)}, u32[]{:S(2)}) collective-permute-start(bf16[8,6144]{1,0:T(8,128)(2,1)S(1)} %collective-permute-done.far_ref), channel_id=1, source_target_pairs={{0,4},{2,6},{4,0},{6,2},{8,12},{10,14},{12,8},{14,10},{1,5},{3,7},... | collective-permute-start | bytes 294920 | tf_op jit(solution)/shard_map/ppermute | solution.py:175
  12.3 4.6 %collective-permute-start.1 = (bf16[8,6144]{1,0:T(8,128)(2,1)S(1)}, bf16[8,6144]{1,0:T(8,128)(2,1)S(1)}, u32[]{:S(2)}, u32[]{:S(2)}) collective-permute-start(bf16[8,6144]{1,0:T(8,128)(2,1)S(1)} %collective-permute-done.far_ref), channel_id=1, source_target_pairs={{0,2},{2,0},{4,6},{6,4},{8,10},{10,8},{12,14},{14,12},{1,3},{3,1},... | collective-permute-start | bytes 294920 | tf_op jit(solution)/shard_map/ppermute | solution.py:175
  18.3 1.2 %collective-permute-start.7 = (f32[24,128]{1,0:T(8,128)S(1)}, f32[24,128]{1,0:T(8,128)S(1)}, u32[]{:S(2)}, u32[]{:S(2)}) collective-permute-start(f32[24,128]{1,0:T(8,128)S(1)} %get-tuple-element.16), channel_id=1, source_target_pairs={{0,1},{1,0},{2,3},{3,2},{4,5},{5,4},{6,7},{7,6},{8,9},{9,8},{10,11... | collective-permute-start | bytes 36872 | tf_op jit(solution)/shard_map/ppermute | solution.py:208

commit v3 on v2

--- a/solution.py
+++ b/solution.py
@@ -9,6 +9,8 @@
 
 LANES = 256
 PACKED = 8
+REST = jnp.float8_e5m2
+REST_SCALE = 8192.0
 CONTRACT_LAST = (((1,), (1,)), ((), ()))
 VMEM_LIMIT = 40 * 1024 * 1024
 
@@ -63,8 +65,8 @@
     return lax.dynamic_slice_in_dim(summed, lax.axis_index("dim") * half_cols, half_cols, 1)
 
 
-def fold_kernel(train_ref, precond_ref, folded_ref):
-    train_rows, dims = train_ref.shape
+def fold_kernel(train_ref, precond_ref, head_ref, rest_ref):
+    dims = train_ref.shape[1]
     block = precond_ref.shape[0]
     row_block = lax.broadcasted_iota(jnp.int32, (LANES, LANES), 0) // block
     col_block = lax.broadcasted_iota(jnp.int32, (LANES, LANES), 1) // block
@@ -75,9 +77,8 @@
         matrix = jnp.where(diagonal, stacked, jnp.zeros_like(stacked))
         value = jnp.dot(train_ref[:, at], matrix, preferred_element_type=jnp.float32)
         head = value.astype(jnp.bfloat16)
-        folded_ref[0:train_rows, at] = head
-        rest = value - head.astype(jnp.float32)
-        folded_ref[train_rows : 2 * train_rows, at] = rest.astype(jnp.bfloat16)
+        head_ref[:, at] = head
+        rest_ref[:, at] = ((value - head.astype(jnp.float32)) * REST_SCALE).astype(REST)
 
 
 def pack_kernel(queries_ref, packed_ref):
@@ -93,35 +94,32 @@
     packed_ref[...] = jnp.concatenate([main, below], 0).astype(jnp.bfloat16)
 
 
-def partial_scores(folded_ref, refs):
+def rows_by_train(rows, head_ref, rest_ref, at):
+    head = lax.dot_general(
+        rows.astype(jnp.bfloat16), head_ref[:, at], CONTRACT_LAST, preferred_element_type=jnp.float32
+    )
+    rest = lax.dot_general(
+        rows.astype(REST), rest_ref[:, at], CONTRACT_LAST, preferred_element_type=jnp.float32
+    )
+    return head + rest * (1.0 / REST_SCALE)
+
+
+def partial_scores(head_ref, rest_ref, refs):
     width = refs[0].shape[1]
-    dims = folded_ref.shape[1]
+    dims = head_ref.shape[1]
     tail = dims - width
     each = width // tail
     rows = width * PACKED // dims
     joined = jnp.concatenate([r[...].astype(jnp.float32) for r in refs], 0)
     tails = jnp.concatenate([joined[:, m * tail : (m + 1) * tail] for m in range(each)], 0)
-    main = lax.dot_general(
-        joined.astype(jnp.bfloat16),
-        folded_ref[:, :width],
-        CONTRACT_LAST,
-        preferred_element_type=jnp.float32,
-    )
-    rest = lax.dot_general(
-        tails.astype(jnp.bfloat16),
-        folded_ref[:, width:],
-        CONTRACT_LAST,
-        preferred_element_type=jnp.float32,
-    )
-    train_rows = main.shape[1] // 2
-    main = main[:, :train_rows] + main[:, train_rows:]
-    rest = rest[:, :train_rows] + rest[:, train_rows:]
+    main = rows_by_train(joined, head_ref, rest_ref, pl.ds(0, width))
+    tails = rows_by_train(tails, head_ref, rest_ref, pl.ds(width, tail))
     scores = []
     for i in range(len(refs)):
         below = []
         for row in range(rows):
             at = (row % each * len(refs) + i) * PACKED + rows + row // each
-            below.append(rest[at : at + 1])
+            below.append(tails[at : at + 1])
         scores.append(main[i * PACKED : i * PACKED + rows] + jnp.concatenate(below, 0))
     return scores
 
@@ -136,14 +134,14 @@
     return jnp.concatenate(placed, 0)
 
 
-def near_kernel(folded_ref, own_ref, xz_ref, z_ref, x_ref, far_ref, near_ref, first_ref):
-    pieces = partial_scores(folded_ref, (own_ref, x_ref, z_ref, xz_ref, far_ref))
+def near_kernel(head_ref, rest_ref, own_ref, xz_ref, x_ref, z_ref, far_ref, near_ref, first_ref):
+    pieces = partial_scores(head_ref, rest_ref, (own_ref, x_ref, z_ref, xz_ref, far_ref))
     near_ref[...] = in_order(pieces[:4], lax.rem(lax.axis_index("ex"), 4))
     first_ref[...] = pieces[4]
 
 
-def far_kernel(folded_ref, x_ref, z_ref, y_ref, near_ref, first_ref, keep_ref, send_ref):
-    pieces = [first_ref[...]] + partial_scores(folded_ref, (x_ref, z_ref, y_ref))
+def far_kernel(head_ref, rest_ref, x_ref, z_ref, y_ref, near_ref, first_ref, keep_ref, send_ref):
+    pieces = [first_ref[...]] + partial_scores(head_ref, rest_ref, (x_ref, z_ref, y_ref))
     place = lax.axis_index("ex")
     flip = lax.rem(place, 4)
     flip = flip ^ jnp.where(lax.axis_index("grp") == 1, 2, 1)
@@ -185,13 +183,16 @@
         5_000_000_000,
     )
     far = swap_both(own, lambda g, e: g * 8 + (e ^ (6 if g else 5)))
-    folded = call(
+    head, rest = call(
         fold_kernel,
-        jax.ShapeDtypeStruct((2 * train_rows, dims), jnp.bfloat16),
+        (
+            jax.ShapeDtypeStruct((train_rows, dims), jnp.bfloat16),
+            jax.ShapeDtypeStruct((train_rows, dims), REST),
+        ),
         (train_grads, precond.T),
         2 * train_rows * dims * LANES,
     )
-    far, folded = lax.optimization_barrier((far, folded))
+    far, head, rest = lax.optimization_barrier((far, head, rest))
     far_x = swap(far, 1)
     far_z = swap(far, 2)
     far_y = lax.ppermute(far, "grp", [(0, 1), (1, 0)])
@@ -202,9 +203,9 @@
     half = jax.ShapeDtypeStruct((query_rows * 4, train_rows), jnp.float32)
     flops = 4 * train_rows * dims * LANES
     near, first = call(
-        near_kernel, (half, quarter), (folded, own, near_xz, near_z, near_x, far), flops
-    )
-    keep, send = call(far_kernel, (half, half), (folded, far_x, far_z, far_y, near, first), flops)
+        near_kernel, (half, quarter), (head, rest, own, near_xz, near_x, near_z, far), flops
+    )
+    keep, send = call(far_kernel, (half, half), (head, rest, far_x, far_z, far_y, near, first), flops)
     return (keep + lax.ppermute(send, "dim", [(0, 1), (1, 0)])).T
 
 

time: 20.3 us -> 20 us (0.985)
  Pallas kernels: 3.73 us -> 3.13 us
    pallas_call x4, Pallas kernels: 3.73 us -> 3.13 us  [call(): pl.pallas_call(kernel, out_shape=outs, in_specs=[vmem] * len(args), out_s...]
    ppermute x5, waiting for transfers between devices: 1.71 us -> 2.13 us  [swap(): return lax.ppermute(value, 'ex', [(i, i ^ mask) for i in range(8)])]
    ppermute x1, starting transfers between devices: 1.07 us -> 1.36 us  [crossing_scores(): far_y = lax.ppermute(far, 'grp', [(0, 1), (1, 0)])]
    ppermute x1, waiting for transfers between devices: 0.6 us -> 0.32 us  [swap_both(): return lax.ppermute(value, ('grp', 'ex'), route)]
  transfers between devices with their start and end apart: 8 -> 8, of which waited for: 5 -> 4; matrix products, arithmetic and copies ran while one was open for 0% -> 0% of each run, Pallas kernels for 12% -> 10%
where the time goes in v3:
time: 20 us; the launch traced here: 19.8 us
  starting transfers between devices  11.4 us (57%)
  waiting for transfers between devices  3.62 us (18%)
  Pallas kernels  3.13 us (16%)
  local copies, waits for them, and re-layouts  1 us (5%)
  other arithmetic  0.6 us (3%)
    ppermute x1, starting transfers between devices, swap_both(): return lax.ppermute(value, ('grp', 'ex'), route)  5.03 us
    ppermute x5, starting transfers between devices, swap(): return lax.ppermute(value, 'ex', [(i, i ^ mask) for i in range(8)])  4.98 us
    pallas_call x4, Pallas kernels, call(): pl.pallas_call(kernel, out_shape=outs, in_specs=[vmem] * len(args), out_s...  3.13 us
    ppermute x5, waiting for transfers between devices, swap(): return lax.ppermute(value, 'ex', [(i, i ^ mask) for i in range(8)])  2.13 us
    ppermute x1, starting transfers between devices, crossing_scores(): far_y = lax.ppermute(far, 'grp', [(0, 1), (1, 0)])  1.36 us
    ppermute x1, waiting for transfers between devices, crossing_scores(): return (keep + lax.ppermute(send, 'dim', [(0, 1), (1, 0)])).T  1.16 us
    unnamed x6, local copies, waits for them, and re-layouts  1 us
    transpose x1, other arithmetic, crossing_scores(): return (keep + lax.ppermute(send, 'dim', [(0, 1), (1, 0)])).T  0.6 us
  transfers between devices with their start and end apart: 8, of which 4 were waited for; matrix products, arithmetic and copies ran while one was open for 0% of the time, Pallas kernels for 10%

profile of v3, /device:TPU:0, one launch (start us, length us, event | category | flops | bytes accessed | tf_op | source)
XLA Modules:
  0.0 19.8 jit_solution(286169201849838884)
XLA Ops:
  0.0 0.0 copy-start.1
  0.0 0.0 copy-start.2
  0.0 1.0 %copy-done.2 = bf16[6,8192]{1,0:T(8,128)(2,1)S(1)} copy-done((bf16[6,8192]{1,0:T(8,128)(2,1)S(1)}, bf16[6,8192]{1,0:T(8,128)(2,1)}, u32[]{:S(2)}) %copy-start.2) | copy-done | bytes 98328
  1.0 0.0 copy-start
  1.0 5.0 %collective-permute-start = (bf16[8,6144]{1,0:T(8,128)(2,1)S(1)}, bf16[8,6144]{1,0:T(8,128)(2,1)S(1)}, u32[]{:S(2)}, u32[]{:S(2)}) collective-permute-start(bf16[8,6144]{1,0:T(8,128)(2,1)S(1)} %shard_map.37.own_ref), channel_id=1, source_target_pairs={{0,10},{2,8},{4,14},{6,12},{8,2},{10,0},{12,6},{14,4},{16,28},{18,... | collective-permute-start | bytes 294920 | tf_op jit(solution)/shard_map/ppermute | solution.py:177
  6.1 1.6 %collective-permute-start.6 = (bf16[8,6144]{1,0:T(8,128)(2,1)S(1)}, bf16[8,6144]{1,0:T(8,128)(2,1)S(1)}, u32[]{:S(2)}, u32[]{:S(2)}) collective-permute-start(bf16[8,6144]{1,0:T(8,128)(2,1)S(1)} %shard_map.37.own_ref), channel_id=1, source_target_pairs={{0,4},{2,6},{4,0},{6,2},{8,12},{10,14},{12,8},{14,10},{1,5},{3,7},... | collective-permute-start | bytes 294920 | tf_op jit(solution)/shard_map/ppermute | solution.py:173
  7.7 0.5 %collective-permute-start.5 = (bf16[8,6144]{1,0:T(8,128)(2,1)S(1)}, bf16[8,6144]{1,0:T(8,128)(2,1)S(1)}, u32[]{:S(2)}, u32[]{:S(2)}) collective-permute-start(bf16[8,6144]{1,0:T(8,128)(2,1)S(1)} %shard_map.37.own_ref), channel_id=1, source_target_pairs={{0,2},{2,0},{4,6},{6,4},{8,10},{10,8},{12,14},{14,12},{1,3},{3,1},... | collective-permute-start | bytes 294920 | tf_op jit(solution)/shard_map/ppermute | solution.py:173
  8.2 1.4 %collective-permute-start.4 = (bf16[8,6144]{1,0:T(8,128)(2,1)S(1)}, bf16[8,6144]{1,0:T(8,128)(2,1)S(1)}, u32[]{:S(2)}, u32[]{:S(2)}) collective-permute-start(bf16[8,6144]{1,0:T(8,128)(2,1)S(1)} %shard_map.37.own_ref), channel_id=1, source_target_pairs={{0,6},{2,4},{4,2},{6,0},{8,14},{10,12},{12,10},{14,8},{1,7},{3,5},... | collective-permute-start | bytes 294920 | tf_op jit(solution)/shard_map/ppermute | solution.py:173
  9.6 0.0 copy-done.1
  9.6 0.0 copy-done
  9.6 1.0 %shard_map.38 = (bf16[128,8192]{1,0:T(8,128)(2,1)S(1)}, f8e5m2[128,8192]{1,0:T(32,128)(4,1)S(1)}) custom-call(bf16[128,8192]{1,0:T(8,128)(2,1)S(1)} %copy-done, bf16[64,8192]{1,0:T(8,128)(2,1)S(1)} %bitcast.3), custom_call_target="tpu_custom_call" | custom-call | flops 536870912 | bytes 3145728 | tf_op jit(solution)/shard_map/pallas_call | solution.py:158
  10.6 0.3 %collective-permute-done.far_ref = bf16[8,6144]{1,0:T(8,128)(2,1)S(1)} collective-permute-done((bf16[8,6144]{1,0:T(8,128)(2,1)S(1)}, bf16[8,6144]{1,0:T(8,128)(2,1)S(1)}, u32[]{:S(2)}, u32[]{:S(2)}) %collective-permute-start) | collective-permute-done | bytes 98336 | tf_op jit(solution)/shard_map/ppermute | solution.py:177
  10.9 1.4 %collective-permute-start.3 = (bf16[8,6144]{1,0:T(8,128)(2,1)S(1)}, bf16[8,6144]{1,0:T(8,128)(2,1)S(1)}, u32[]{:S(2)}, u32[]{:S(2)}) collective-permute-start(bf16[8,6144]{1,0:T(8,128)(2,1)S(1)} %collective-permute-done.far_ref), channel_id=1, source_target_pairs={{0,16},{16,0},{1,17},{17,1},{2,18},{18,2},{3,19},{19,3},{4,20},{20... | collective-permute-start | bytes 294920 | tf_op jit(solution)/shard_map/ppermute | solution.py:198
  12.3 0.0 collective-permute-start.2
  12.3 0.0 collective-permute-done.6.z_ref
  12.3 1.4 %collective-permute-start.1 = (bf16[8,6144]{1,0:T(8,128)(2,1)S(1)}, bf16[8,6144]{1,0:T(8,128)(2,1)S(1)}, u32[]{:S(2)}, u32[]{:S(2)}) collective-permute-start(bf16[8,6144]{1,0:T(8,128)(2,1)S(1)} %collective-permute-done.far_ref), channel_id=1, source_target_pairs={{0,2},{2,0},{4,6},{6,4},{8,10},{10,8},{12,14},{14,12},{1,3},{3,1},... | collective-permute-start | bytes 294920 | tf_op jit(solution)/shard_map/ppermute | solution.py:173
  13.8 0.9 %collective-permute-done.5.x_ref = bf16[8,6144]{1,0:T(8,128)(2,1)S(1)} collective-permute-done((bf16[8,6144]{1,0:T(8,128)(2,1)S(1)}, bf16[8,6144]{1,0:T(8,128)(2,1)S(1)}, u32[]{:S(2)}, u32[]{:S(2)}) %collective-permute-start.5) | collective-permute-done | bytes 98336 | tf_op jit(solution)/shard_map/ppermute | solution.py:173
  14.7 0.0 collective-permute-done.4.xz_ref
  14.7 1.0 %shard_map.39 = (f32[24,128]{1,0:T(8,128)S(1)}, f32[6,128]{1,0:T(8,128)S(1)}) custom-call(bf16[128,8192]{1,0:T(8,128)(2,1)S(1)} %get-tuple-element.16.head_ref, f8e5m2[128,8192]{1,0:T(32,128)(4,1)S(1)} %get-tuple-element.17.rest_ref, bf16[8,6144]{1,0:T(8,128)(2,1)S(1)} %shard_map.37.own_ref, bf16[8,6144]{1,0:T(8,128)(2,1)S(1)} %collective-permute-done.4.xz_ref, ...), custom_call_target="tpu_custom_call" | custom-call | flops 1073741824 | bytes 3637248 | tf_op jit(solution)/shard_map/pallas_call | solution.py:158
  15.8 0.0 collective-permute-done.3.y_ref
  15.8 1.1 %collective-permute-done.2.z_ref = bf16[8,6144]{1,0:T(8,128)(2,1)S(1)} collective-permute-done((bf16[8,6144]{1,0:T(8,128)(2,1)S(1)}, bf16[8,6144]{1,0:T(8,128)(2,1)S(1)}, u32[]{:S(2)}, u32[]{:S(2)}) %collective-permute-start.2) | collective-permute-done | bytes 98336 | tf_op jit(solution)/shard_map/ppermute | solution.py:173
  16.9 0.1 collective-permute-done.1.x_ref
  17.0 1.0 %shard_map.40 = (f32[24,128]{1,0:T(8,128)S(1)}, f32[24,128]{1,0:T(8,128)S(1)}) custom-call(bf16[128,8192]{1,0:T(8,128)(2,1)S(1)} %get-tuple-element.16.head_ref, f8e5m2[128,8192]{1,0:T(32,128)(4,1)S(1)} %get-tuple-element.17.rest_ref, bf16[8,6144]{1,0:T(8,128)(2,1)S(1)} %collective-permute-done.1.x_ref, bf16[8,6144]{1,0:T(8,128)(2,1)S(1)} %collective-permute-done.2.z_ref, ...), custom_call_target="tpu_custom_call" | custom-call | flops 1073741824 | bytes 3456000 | tf_op jit(solution)/shard_map/pallas_call | solution.py:158
  18.0 0.1 collective-permute-start.7
  18.1 1.2 %collective-permute-done.7 = f32[24,128]{1,0:T(8,128)S(1)} collective-permute-done((f32[24,128]{1,0:T(8,128)S(1)}, f32[24,128]{1,0:T(8,128)S(1)}, u32[]{:S(2)}, u32[]{:S(2)}) %collective-permute-start.7) | collective-permute-done | bytes 12320 | tf_op jit(solution)/shard_map/ppermute | solution.py:209
  19.2 0.6 %add_bitcast_fusion = f32[128,24]{0,1:T(8,128)} fusion(f32[24,128]{1,0:T(8,128)S(1)} %get-tuple-element.21, f32[24,128]{1,0:T(8,128)S(1)} %collective-permute-done.7), kind=kLoop, calls=%fused_computation | loop fusion | flops 3072 | bytes 36864 | tf_op jit(solution)/shard_map/transpose | solution.py:209
  (1 shorter events, 0.0 us)
Async XLA Ops:
  0.0 9.6 %copy-start.1 = (bf16[8192,64]{0,1:T(8,128)(2,1)S(1)}, bf16[8192,64]{0,1:T(8,128)(2,1)}, u32[]{:S(2)}) copy-start(bf16[8192,64]{0,1:T(8,128)(2,1)} %param.5) | copy-start | bytes 3145732
  0.0 1.0 %copy-start.2 = (bf16[6,8192]{1,0:T(8,128)(2,1)S(1)}, bf16[6,8192]{1,0:T(8,128)(2,1)}, u32[]{:S(2)}) copy-start(bf16[6,8192]{1,0:T(8,128)(2,1)} %queries_ref.1) | copy-start | bytes 294916
  1.0 8.6 %copy-start = (bf16[128,8192]{1,0:T(8,128)(2,1)S(1)}, bf16[128,8192]{1,0:T(8,128)(2,1)}, u32[]{:S(2)}) copy-start(bf16[128,8192]{1,0:T(8,128)(2,1)} %train_ref.1) | copy-start | bytes 6291460
  1.0 9.9 %collective-permute-start = (bf16[8,6144]{1,0:T(8,128)(2,1)S(1)}, bf16[8,6144]{1,0:T(8,128)(2,1)S(1)}, u32[]{:S(2)}, u32[]{:S(2)}) collective-permute-start(bf16[8,6144]{1,0:T(8,128)(2,1)S(1)} %shard_map.37.own_ref), channel_id=1, source_target_pairs={{0,10},{2,8},{4,14},{6,12},{8,2},{10,0},{12,6},{14,4},{16,28},{18,... | collective-permute-start | bytes 294920 | tf_op jit(solution)/shard_map/ppermute | solution.py:177
  6.1 6.3 %collective-permute-start.6 = (bf16[8,6144]{1,0:T(8,128)(2,1)S(1)}, bf16[8,6144]{1,0:T(8,128)(2,1)S(1)}, u32[]{:S(2)}, u32[]{:S(2)}) collective-permute-start(bf16[8,6144]{1,0:T(8,128)(2,1)S(1)} %shard_map.37.own_ref), channel_id=1, source_target_pairs={{0,4},{2,6},{4,0},{6,2},{8,12},{10,14},{12,8},{14,10},{1,5},{3,7},... | collective-permute-start | bytes 294920 | tf_op jit(solution)/shard_map/ppermute | solution.py:173
  7.7 7.1 %collective-permute-start.5 = (bf16[8,6144]{1,0:T(8,128)(2,1)S(1)}, bf16[8,6144]{1,0:T(8,128)(2,1)S(1)}, u32[]{:S(2)}, u32[]{:S(2)}) collective-permute-start(bf16[8,6144]{1,0:T(8,128)(2,1)S(1)} %shard_map.37.own_ref), channel_id=1, source_target_pairs={{0,2},{2,0},{4,6},{6,4},{8,10},{10,8},{12,14},{14,12},{1,3},{3,1},... | collective-permute-start | bytes 294920 | tf_op jit(solution)/shard_map/ppermute | solution.py:173
  8.2 6.6 %collective-permute-start.4 = (bf16[8,6144]{1,0:T(8,128)(2,1)S(1)}, bf16[8,6144]{1,0:T(8,128)(2,1)S(1)}, u32[]{:S(2)}, u32[]{:S(2)}) collective-permute-start(bf16[8,6144]{1,0:T(8,128)(2,1)S(1)} %shard_map.37.own_ref), channel_id=1, source_target_pairs={{0,6},{2,4},{4,2},{6,0},{8,14},{10,12},{12,10},{14,8},{1,7},{3,5},... | collective-permute-start | bytes 294920 | tf_op jit(solution)/shard_map/ppermute | solution.py:173
  10.9 4.8 %collective-permute-start.3 = (bf16[8,6144]{1,0:T(8,128)(2,1)S(1)}, bf16[8,6144]{1,0:T(8,128)(2,1)S(1)}, u32[]{:S(2)}, u32[]{:S(2)}) collective-permute-start(bf16[8,6144]{1,0:T(8,128)(2,1)S(1)} %collective-permute-done.far_ref), channel_id=1, source_target_pairs={{0,16},{16,0},{1,17},{17,1},{2,18},{18,2},{3,19},{19,3},{4,20},{20... | collective-permute-start | bytes 294920 | tf_op jit(solution)/shard_map/ppermute | solution.py:198
  12.3 4.6 %collective-permute-start.2 = (bf16[8,6144]{1,0:T(8,128)(2,1)S(1)}, bf16[8,6144]{1,0:T(8,128)(2,1)S(1)}, u32[]{:S(2)}, u32[]{:S(2)}) collective-permute-start(bf16[8,6144]{1,0:T(8,128)(2,1)S(1)} %collective-permute-done.far_ref), channel_id=1, source_target_pairs={{0,4},{2,6},{4,0},{6,2},{8,12},{10,14},{12,8},{14,10},{1,5},{3,7},... | collective-permute-start | bytes 294920 | tf_op jit(solution)/shard_map/ppermute | solution.py:173
  12.3 4.6 %collective-permute-start.1 = (bf16[8,6144]{1,0:T(8,128)(2,1)S(1)}, bf16[8,6144]{1,0:T(8,128)(2,1)S(1)}, u32[]{:S(2)}, u32[]{:S(2)}) collective-permute-start(bf16[8,6144]{1,0:T(8,128)(2,1)S(1)} %collective-permute-done.far_ref), channel_id=1, source_target_pairs={{0,2},{2,0},{4,6},{6,4},{8,10},{10,8},{12,14},{14,12},{1,3},{3,1},... | collective-permute-start | bytes 294920 | tf_op jit(solution)/shard_map/ppermute | solution.py:173
  18.0 1.2 %collective-permute-start.7 = (f32[24,128]{1,0:T(8,128)S(1)}, f32[24,128]{1,0:T(8,128)S(1)}, u32[]{:S(2)}, u32[]{:S(2)}) collective-permute-start(f32[24,128]{1,0:T(8,128)S(1)} %get-tuple-element.22), channel_id=1, source_target_pairs={{0,1},{1,0},{2,3},{3,2},{4,5},{5,4},{6,7},{7,6},{8,9},{9,8},{10,11... | collective-permute-start | bytes 36872 | tf_op jit(solution)/shard_map/ppermute | solution.py:209
